TPU v7x, 128 devices: a whole 4x4x4 slice. The times are simulated.
128 devices in a mesh: ctx: 32 (over y, x, core), head: 4 (over z).
Axes of the slice: x: 4, y: 4, z: 4, core: 2. Of those that a mesh axis runs over, the one named last changes fastest.
Arguments:
- queries: bfloat16 [49152, 3072], P('ctx', 'head'), may hold values from -6 to 6
- keys: bfloat16 [49152, 3072], P('ctx', 'head'), may hold values from -6 to 6
- values: bfloat16 [49152, 3072], P('ctx', 'head'), may hold values from -40 to 40
- log_decay: float32 [49152, 32], P('ctx', 'head'), may hold values from -0.75 to 0, as said below
- gain: float32 [3072], P('head'), may hold values from 0.5 to 1.5
- d_out: bfloat16 [49152, 3072], P('ctx', 'head'), may hold values from -6 to 6
Outputs:
- layer_out: bfloat16 [49152, 3072], P('ctx', 'head')
- d_queries: bfloat16 [49152, 3072], P('ctx', 'head')
- d_keys: bfloat16 [49152, 3072], P('ctx', 'head')
- d_values: bfloat16 [49152, 3072], P('ctx', 'head')
- d_gain: float32 [3072], P('head')
Inputs may be any that keep to these rules, and one draw needn't show every extreme that they name: `log_decay`: every entry is negative.
All inputs are finite; a program needn't handle non-finite values.
Results may differ from a plain program's by a relative error of at most 0.0018.
Values sent between devices are 32-bit elements; how exact they have to be, the bound alone decides.
A program may use at most 192 MiB of HBM per device.

v0:
```python
import functools

import jax
import jax.numpy as jnp
from jax import lax
from jax.experimental import pallas as pl
from jax.experimental.pallas import tpu as pltpu
from jax.sharding import PartitionSpec as P

F32 = jnp.float32
BF16 = jnp.bfloat16
C = 128
HS = 96
GL = 384
PIECES = 3
OWNERS = 24
NEG = -1e30
LOG2E = 1.4426950408889634
MESH = pl.DeviceIdType.MESH


def dot(a, b):
    return lax.dot_general(a, b, (((1,), (0,)), ((), ())), preferred_element_type=F32)


def dot_nt(a, b):
    return lax.dot_general(a, b, (((1,), (1,)), ((), ())), preferred_element_type=F32)


def both(hi, lo, w):
    r = dot(jnp.concatenate([hi, lo], axis=0), w)
    return r[: hi.shape[0]] + r[hi.shape[0] :]


def both_nt(hi, lo, w):
    r = dot_nt(jnp.concatenate([hi, lo], axis=0), w)
    return r[: hi.shape[0]] + r[hi.shape[0] :]


def split(x):
    hi = x.astype(BF16)
    lo = (x - hi.astype(F32)).astype(BF16)
    return hi, lo


def lane_mask(lo, hi, rows, dtype):
    lane = lax.broadcasted_iota(jnp.int32, (rows, 128), 1)
    return jnp.where((lane >= lo) & (lane < hi), 1.0, 0.0).astype(dtype)


def head_tiles(x, parity, dtype):
    rows = x.shape[0]
    t0, t1 = x[:, :128], x[:, 128:]
    zero = jnp.zeros((rows, 128), dtype)
    if parity == 0:
        a = [t0 * lane_mask(0, 96, rows, dtype), zero]
        b = [t0 * lane_mask(96, 128, rows, dtype), t1 * lane_mask(0, 64, rows, dtype)]
    else:
        a = [t0 * lane_mask(64, 128, rows, dtype), t1 * lane_mask(0, 32, rows, dtype)]
        b = [zero, t1 * lane_mask(32, 128, rows, dtype)]
    return jnp.concatenate(a, axis=1), jnp.concatenate(b, axis=1)


def stacked(x, parity):
    a, b = head_tiles(x, parity, x.dtype)
    return jnp.concatenate([a, b], axis=0)


def block_state(s, parity):
    a, b = head_tiles(s, parity, s.dtype)
    pad = jnp.zeros((64, 256), s.dtype)
    return jnp.concatenate([a, b, pad] if parity == 0 else [pad, a, b], axis=0)


def compact(u, parity):
    a, _ = head_tiles(u[:HS], parity, F32)
    _, b = head_tiles(u[HS:], parity, F32)
    return a + b


def merge(w0, w1):
    return jnp.concatenate([w0[:, :128], w0[:, 128:] + w1[:, :128], w1[:, 128:]], axis=1)


def group_lanes(cols):
    rows = cols[0].shape[0]
    lane = lax.broadcasted_iota(jnp.int32, (rows, 128), 1)
    return jnp.concatenate(
        [
            jnp.where(lane < 96, cols[0], cols[1]),
            jnp.where(lane < 64, cols[1], cols[2]),
            jnp.where(lane < 32, cols[2], cols[3]),
        ],
        axis=1,
    )


def columns_of(ct):
    full = jnp.concatenate([ct, jnp.zeros((C - 8, C), F32)], axis=0).T
    return [jnp.broadcast_to(full[:, h : h + 1], (C, C)) for h in range(8)]


def window(parity):
    return slice(128 * parity, 128 * parity + 256)


def causal_bias(transposed):
    row = lax.broadcasted_iota(jnp.int32, (C, C), 0)
    col = lax.broadcasted_iota(jnp.int32, (C, C), 1)
    keep = row <= col if transposed else row >= col
    return jnp.where(keep, 0.0, NEG)


def pair_decay(ct, cols, heads, bias):
    parts = [jnp.exp2(cols[h] - ct[h : h + 1, :] + bias) for h in heads]
    return jnp.concatenate(parts, axis=1)


def pair_decay_t(ct, cols, heads, bias):
    parts = [jnp.exp2(ct[h : h + 1, :] - cols[h] + bias) for h in heads]
    return jnp.concatenate(parts, axis=1)


def token_sums(x):
    acc = x[:, :128]
    for i in range(1, 6):
        acc = acc + x[:, 128 * i : 128 * i + 128]
    return jnp.sum(acc.T, axis=0, keepdims=True)


def wait_bytes(ref, sem):
    pltpu.make_async_copy(ref, ref, sem).wait()


def owner_of(device):
    return (device // 4) * 3 + jnp.minimum(lax.rem(device, 4), 2)


class Scan:
    def __init__(self, count, me, reverse, send, taken, made, given, sems):
        self.count, self.me, self.reverse = count, me, reverse
        self.send, self.taken, self.made, self.given, self.sems = send, taken, made, given, sems
        self.is_owner = lax.rem(me, 4) != 3
        self.mine = owner_of(me)

    def start(self, state_ref, tot_ref):
        for o in range(OWNERS):
            r, half = o // 2, o % 2
            self.send[o, :, :GL] = state_ref[8 * r : 8 * r + 8, GL * half : GL * half + GL]
            tot = tot_ref[4 * half : 4 * half + 4, :]
            self.send[o, :, GL:] = jnp.concatenate([tot, tot], axis=0)

        @pl.loop(1, self.count)
        def _(i):
            target = lax.rem(self.me + i, self.count)

            @pl.when(lax.rem(target, 4) != 3)
            def _():
                pltpu.make_async_remote_copy(
                    src_ref=self.send.at[owner_of(target)], dst_ref=self.taken.at[self.me],
                    send_sem=self.sems.at[0], recv_sem=self.sems.at[1],
                    device_id={"ctx": target}, device_id_type=MESH,
                ).start()

    def middle(self):
        count, me, mine = self.count, self.me, self.mine

        @pl.when(self.is_owner)
        def _():
            self.taken[me] = self.send[mine]
            wait_bytes(self.taken.at[pl.ds(0, count - 1)], self.sems.at[1])

            def step(i, acc):
                j = count - 1 - i if self.reverse else i
                self.made[j] = acc
                rows = [jnp.broadcast_to(self.taken[j, h : h + 1, GL:], (8, 128)) for h in range(4)]
                return jnp.exp2(group_lanes(rows)) * acc + self.taken[j, :, :GL]

            lax.fori_loop(0, count, step, jnp.zeros((8, GL), F32), unroll=4)

            @pl.loop(1, count)
            def _(i):
                target = lax.rem(me + i, count)
                pltpu.make_async_remote_copy(
                    src_ref=self.made.at[target], dst_ref=self.given.at[mine],
                    send_sem=self.sems.at[2], recv_sem=self.sems.at[3],
                    device_id={"ctx": target}, device_id_type=MESH,
                ).start()

            self.given[mine] = self.made[me]

    def finish(self, out_ref):
        @pl.when(self.is_owner)
        def _():
            wait_bytes(self.given.at[pl.ds(0, OWNERS - 1)], self.sems.at[3])
            wait_bytes(self.send.at[pl.ds(0, OWNERS - 1)], self.sems.at[0])
            wait_bytes(self.made.at[pl.ds(0, self.count - 1)], self.sems.at[2])

        @pl.when(jnp.logical_not(self.is_owner))
        def _():
            wait_bytes(self.given, self.sems.at[3])
            wait_bytes(self.send, self.sems.at[0])

        for o in range(OWNERS):
            r, half = o // 2, o % 2
            out_ref[8 * r : 8 * r + 8, GL * half : GL * half + GL] = self.given[o]


def layer_kernel(
    shards, head_shards, total_width, chunks, q_in, k_in, v_in, do_in, gain_ref, ld_ref,
    out_ref, dq_ref, dk_ref, dv_ref, dgain_ref,
    q_s, k_s, v_s, do_s, in_sems, ct_s, cexp_s, att_s, u_s, shi_s, slo_s, ghi_s, glo_s, ehi_s, elo_s,
    dv_s, own_s, tot_s, run_s, start_s, dg_s, sums_s, sums_t, sums_sems,
    gsend, gtaken, gsems, *scan_refs,
):
    remote = shards > 1
    dk_s = att_s
    if remote:
        me, my_head = lax.axis_index("ctx"), lax.axis_index("head")
        on = Scan(shards, me, False, *scan_refs[:5])
        back = Scan(shards, me, True, *scan_refs[5:])
        barrier = pltpu.get_barrier_semaphore()

        @pl.loop(1, shards)
        def _(i):
            pl.semaphore_signal(
                barrier, inc=1, device_id={"ctx": lax.rem(me + i, shards)}, device_id_type=MESH
            )

        @pl.loop(1, head_shards)
        def _(i):
            pl.semaphore_signal(
                barrier, inc=1, device_id={"head": lax.rem(my_head + i, head_shards)},
                device_id_type=MESH,
            )

    per = chunks // PIECES
    inputs = [(k_in, k_s), (v_in, v_s), (q_in, q_s), (do_in, do_s)]

    def arrival(a, b):
        rows = pl.ds(b * per * C, per * C)
        return pltpu.make_async_copy(inputs[a][0].at[rows], inputs[a][1].at[rows], in_sems.at[a, b])

    for b in range(PIECES):
        arrival(0, b).start()
        arrival(1, b).start()
    for a in (2, 3):
        for b in range(PIECES):
            arrival(a, b).start()

    def rows_of(i):
        return pl.ds(pl.multiple_of(i * C, C), C)

    groups = [slice(GL * g, GL * (g + 1)) for g in range(2)]

    row = lax.broadcasted_iota(jnp.int32, (C, C), 0)
    col = lax.broadcasted_iota(jnp.int32, (C, C), 1)
    upper = jnp.where(row <= col, 1.0, 0.0)
    ct_s[...] = LOG2E * lax.dot_general(
        ld_ref[...], upper, (((1,), (0,)), ((), ())), preferred_element_type=F32,
        precision=lax.Precision.HIGHEST,
    )
    own_s[...] = jnp.zeros_like(own_s)
    tot_s[...] = jnp.zeros_like(tot_s)

    def ct_of(i):
        return ct_s[pl.ds(pl.multiple_of(i * 8, 8), 8), :]

    def states(i):
        rows = rows_of(i)
        ct = ct_of(i)
        tot_s[...] += jnp.broadcast_to(ct[:, C - 1 : C], (8, 128))
        cols = columns_of(ct)
        for g, lanes in enumerate(groups):
            cexp = group_lanes(cols[4 * g : 4 * g + 4])
            cexp_s[rows, lanes] = cexp
            end = cexp[C - 1 : C, :]
            v_hi, v_lo = split(v_s[rows, lanes].astype(F32) * jnp.exp2(end - cexp))
            v_tail = jnp.concatenate([v_hi, v_lo], axis=0)
            kt = k_s[rows, lanes].T
            parts = []
            for p in range(2):
                kp = kt[192 * p : 192 * p + 192]
                parts.append(compact(dot(jnp.concatenate([kp, kp], axis=1), v_tail[:, window(p)]), p))
            u = merge(*parts)
            u_s[i, :, lanes] = u
            own_s[:, lanes] = jnp.exp2(end) * own_s[:, lanes] + u

    def local_rows(i):
        rows = rows_of(i)
        ct = ct_of(i)
        cols = columns_of(ct)
        bias = causal_bias(False)
        for g, lanes in enumerate(groups):
            q, k, v = q_s[rows, lanes], k_s[rows, lanes], v_s[rows, lanes]
            outs = []
            for p in range(2):
                w = window(p)
                heads = (4 * g + 2 * p, 4 * g + 2 * p + 1)
                scores = dot_nt(q[:, w], stacked(k[:, w], p)) * pair_decay(ct, cols, heads, bias)
                outs.append(both(*split(scores), stacked(v[:, w], p)))
            att_s[rows, lanes] = merge(*outs)

    def whole_rows(i):
        rows = rows_of(i)
        for g, lanes in enumerate(groups):
            q = q_s[rows, lanes]
            cexp = cexp_s[rows, lanes]
            end = cexp[C - 1 : C, :]
            s = run_s[:, lanes]
            s_hi, s_lo = split(s)
            shi_s[i, :, lanes] = s_hi
            slo_s[i, :, lanes] = s_lo
            outs = []
            for p in range(2):
                w = window(p)
                outs.append(dot(q[:, w], block_state(s_hi[:, w], p)) + dot(q[:, w], block_state(s_lo[:, w], p)))
            att_s[rows, lanes] += jnp.exp2(cexp) * merge(*outs)
            run_s[:, lanes] = jnp.exp2(end) * s + u_s[i, :, lanes]
        att = att_s[rows, :]
        grown = do_s[rows, :].astype(F32) * gain_ref[...]
        sums_s[i] = jnp.concatenate(
            [token_sums(att * att), token_sums(grown * att), jnp.zeros((6, C), F32)], axis=0
        )

    def sums_copy(b, target):
        part = pl.ds(b * per, per)
        return pltpu.make_async_remote_copy(
            src_ref=sums_s.at[part], dst_ref=sums_t.at[my_head, part], send_sem=sums_sems.at[0, b],
            recv_sem=sums_sems.at[1, b], device_id={"head": target}, device_id_type=MESH,
        )

    def norm_rows(i):
        rows = rows_of(i)
        if remote:
            sums = sums_t[0, i]
            for j in range(1, head_shards):
                sums = sums + sums_t[j, i]
        else:
            sums = sums_s[i]
        rms = jnp.sqrt(sums[0:1, :] / total_width + 1e-06)
        inv = 1.0 / rms
        mean = sums[1:2, :] * inv / total_width
        inv_c = jnp.broadcast_to(inv, (C, C)).T
        coef_c = jnp.broadcast_to(mean * inv * inv, (C, C)).T
        inv_c = jnp.concatenate([inv_c] * 3, axis=1)
        coef_c = jnp.concatenate([coef_c] * 3, axis=1)
        for g, lanes in enumerate(groups):
            att = att_s[rows, lanes]
            up = do_s[rows, lanes].astype(F32)
            gain = gain_ref[:, lanes]
            normed = att * inv_c
            out_ref[rows, lanes] = (normed * gain).astype(BF16)
            dg_s[:, lanes] += jnp.sum((up * normed).reshape(C // 8, 8, GL), axis=0)
            grad = up * gain * inv_c - att * coef_c
            g_hi, g_lo = split(grad)
            ghi_s[rows, lanes] = g_hi
            glo_s[rows, lanes] = g_lo
            cexp = cexp_s[rows, lanes]
            end = cexp[C - 1 : C, :]
            e_hi, e_lo = split(grad * jnp.exp2(cexp))
            ehi_s[rows, lanes] = e_hi
            elo_s[rows, lanes] = e_lo
            e_both = jnp.concatenate([e_hi, e_lo], axis=0)
            qt = q_s[rows, lanes].T
            parts = []
            for p in range(2):
                qp = qt[192 * p : 192 * p + 192]
                parts.append(compact(dot(jnp.concatenate([qp, qp], axis=1), e_both[:, window(p)]), p))
            w = merge(*parts)
            u_s[i, :, lanes] = w
            own_s[:, lanes] += jnp.exp2(start_s[0:1, lanes]) * w
            start_s[0:1, lanes] += end

    def grad_rows(i):
        rows = rows_of(i)
        ct = ct_of(i)
        cols = columns_of(ct)
        bias, bias_t = causal_bias(False), causal_bias(True)
        for g, lanes in enumerate(groups):
            q, k, v = q_s[rows, lanes], k_s[rows, lanes], v_s[rows, lanes]
            g_hi, g_lo = ghi_s[rows, lanes], glo_s[rows, lanes]
            e_hi, e_lo = ehi_s[rows, lanes], elo_s[rows, lanes]
            s_hi, s_lo = shi_s[i, :, lanes], slo_s[i, :, lanes]
            dqs, dks, dvs = [], [], []
            for p in range(2):
                w = window(p)
                heads = (4 * g + 2 * p, 4 * g + 2 * p + 1)
                qw, kw, vw, hw, lw = q[:, w], k[:, w], v[:, w], g_hi[:, w], g_lo[:, w]
                ks, qs, vs = stacked(kw, p), stacked(qw, p), stacked(vw, p)
                hs, ls = stacked(hw, p), stacked(lw, p)
                decay = pair_decay(ct, cols, heads, bias)
                decay_t = pair_decay_t(ct, cols, heads, bias_t)
                b_hi, b_lo = block_state(s_hi[:, w], p), block_state(s_lo[:, w], p)
                d_hi, d_lo = split(both_nt(hw, lw, vs) * decay)
                dqs.append(
                    both(d_hi, d_lo, ks)
                    + (both_nt(e_hi[:, w], e_lo[:, w], b_hi) + dot_nt(e_hi[:, w], b_lo))
                )
                t_hi, t_lo = split((dot_nt(vw, hs) + dot_nt(vw, ls)) * decay_t)
                dks.append(both(t_hi, t_lo, qs))
                p_hi, p_lo = split(dot_nt(kw, qs) * decay_t)
                dvs.append(both(p_hi, p_lo, hs) + dot(p_hi, ls))
            dq_ref[rows, lanes] = merge(*dqs).astype(BF16)
            dk_s[rows, lanes] = merge(*dks)
            dv_s[rows, lanes] = merge(*dvs)

    def last_rows(i):
        rows = rows_of(i)
        for g, lanes in enumerate(groups):
            k, v = k_s[rows, lanes], v_s[rows, lanes]
            cexp = cexp_s[rows, lanes]
            end = cexp[C - 1 : C, :]
            tail = jnp.exp2(end - cexp)
            s = run_s[:, lanes]
            s_hi, s_lo = split(s)
            dks, dvs = [], []
            for p in range(2):
                w = window(p)
                b_hi, b_lo = block_state(s_hi[:, w], p), block_state(s_lo[:, w], p)
                dks.append(dot_nt(v[:, w], b_hi) + dot_nt(v[:, w], b_lo))
                dvs.append(dot(k[:, w], b_hi) + dot(k[:, w], b_lo))
            dk_ref[rows, lanes] = (dk_s[rows, lanes] + tail * merge(*dks)).astype(BF16)
            dv_ref[rows, lanes] = (dv_s[rows, lanes] + tail * merge(*dvs)).astype(BF16)
            run_s[:, lanes] = jnp.exp2(end) * s + u_s[i, :, lanes]

    def over(lo, hi, f):
        pl.loop(lo, hi)(f)

    for b in range(PIECES):
        arrival(0, b).wait()
        arrival(1, b).wait()
        over(b * per, (b + 1) * per, states)
    if remote:
        pl.semaphore_wait(barrier, shards + head_shards - 2)
        on.start(own_s, tot_s)
    for b in range(PIECES):
        arrival(2, b).wait()
        arrival(3, b).wait()
    split_at = chunks // 2
    over(0, split_at, local_rows)
    if remote:
        on.middle()
    over(split_at, chunks, local_rows)
    if remote:
        on.finish(run_s)
    else:
        run_s[...] = jnp.zeros_like(run_s)
    for b in range(PIECES):
        over(b * per, (b + 1) * per, whole_rows)
        if remote:
            part = pl.ds(b * per, per)
            sums_t[my_head, part] = sums_s[part]

            @pl.loop(1, head_shards)
            def _(i):
                sums_copy(b, lax.rem(my_head + i, head_shards)).start()

    own_s[...] = jnp.zeros_like(own_s)
    start_s[...] = jnp.zeros_like(start_s)
    dg_s[...] = jnp.zeros_like(dg_s)
    for b in range(PIECES):
        if remote:
            moved = sums_t.at[pl.ds(0, head_shards - 1), pl.ds(b * per, per)]
            wait_bytes(moved, sums_sems.at[1, b])
            wait_bytes(moved, sums_sems.at[0, b])
        over(b * per, (b + 1) * per, norm_rows)

    sums = jnp.sum(dg_s[...], axis=0, keepdims=True)
    tile = jnp.concatenate(
        [sums[:, 128 * i : 128 * i + 128] for i in range(6)] + [jnp.zeros((2, 128), F32)], axis=0
    )
    if remote:
        back.start(own_s, tot_s)
        gsend[...] = tile
        gtaken[me] = tile

        @pl.loop(1, shards)
        def _(i):
            pltpu.make_async_remote_copy(
                src_ref=gsend, dst_ref=gtaken.at[me], send_sem=gsems.at[0], recv_sem=gsems.at[1],
                device_id={"ctx": lax.rem(me + i, shards)}, device_id_type=MESH,
            ).start()

    over(0, split_at, grad_rows)
    if remote:
        back.middle()
    over(split_at, chunks, grad_rows)
    if remote:
        wait_bytes(gtaken.at[pl.ds(0, shards - 1)], gsems.at[1])
        wait_bytes(gtaken.at[pl.ds(0, shards - 1)], gsems.at[0])
        dgain_ref[...] = lax.fori_loop(
            0, shards, lambda i, acc: acc + gtaken[i], jnp.zeros((8, 128), F32)
        )
        back.finish(run_s)
    else:
        dgain_ref[...] = tile
        run_s[...] = jnp.zeros_like(run_s)
    over(0, chunks, lambda i: last_rows(chunks - 1 - i))


def body(shards, head_shards, queries, keys, values, log_decay, gain, d_out):
    n, width = queries.shape
    chunks = n // C
    ld_t = log_decay.reshape(chunks, C, 8).transpose(0, 2, 1).reshape(chunks * 8, C)
    hbm, vmem = pl.BlockSpec(memory_space=pl.ANY), pl.BlockSpec(memory_space=pltpu.VMEM)
    rows = lambda dtype: pltpu.VMEM((n, width), dtype)
    scan = [
        pltpu.VMEM((OWNERS, 8, 512), F32),
        pltpu.VMEM((shards, 8, 512), F32),
        pltpu.VMEM((shards, 8, GL), F32),
        pltpu.VMEM((OWNERS, 8, GL), F32),
        pltpu.SemaphoreType.DMA((4,)),
    ]
    scratch = [rows(BF16)] * 4 + [
        pltpu.SemaphoreType.DMA((4, PIECES)),
        pltpu.VMEM((chunks * 8, C), F32),
        rows(F32),
        rows(F32),
        pltpu.VMEM((chunks, HS, width), F32),
        pltpu.VMEM((chunks, HS, width), BF16),
        pltpu.VMEM((chunks, HS, width), BF16),
        rows(BF16), rows(BF16), rows(BF16), rows(BF16),
        rows(F32),
        pltpu.VMEM((HS, width), F32),
        pltpu.VMEM((8, 128), F32),
        pltpu.VMEM((HS, width), F32),
        pltpu.VMEM((8, width), F32),
        pltpu.VMEM((8, width), F32),
        pltpu.VMEM((chunks, 8, C), F32),
        pltpu.VMEM((head_shards, chunks, 8, C), F32),
        pltpu.SemaphoreType.DMA((2, PIECES)),
        pltpu.VMEM((8, 128), F32),
        pltpu.VMEM((shards, 8, 128), F32),
        pltpu.SemaphoreType.DMA((2,)),
    ] + scan + scan
    params = dict(vmem_limit_bytes=VMEM_LIMIT)
    if shards > 1:
        params.update(collective_id=0, has_side_effects=True)
    out = OUT((n, width), BF16)
    outs = pl.pallas_call(
        functools.partial(
            layer_kernel, shards, head_shards, float(width * head_shards), chunks
        ),
        in_specs=[hbm] * 4 + [vmem, vmem],
        out_specs=[vmem] * 5,
        out_shape=[out] * 4 + [jax.ShapeDtypeStruct((8, 128), F32)],
        scratch_shapes=scratch,
        compiler_params=pltpu.CompilerParams(**params),
        name="layer",
    )(queries, keys, values, d_out, gain[None], ld_t)
    return (*outs[:4], outs[4][:6].reshape(width))


VMEM_LIMIT = 60 * 1024 * 1024
OUT = jax.ShapeDtypeStruct


def solution(mesh):
    rows = P("ctx", "head")
    return jax.shard_map(
        functools.partial(body, mesh.shape["ctx"], mesh.shape["head"]),
        mesh=mesh,
        in_specs=(rows, rows, rows, rows, P("head"), rows),
        out_specs=(rows, rows, rows, rows, P("head")),
        check_vma=False,
    )
```

profile of v0, /device:TPU:1, one launch (start us, length us, event | category | flops | bytes accessed | tf_op | source)
XLA Modules:
  0.0 90.7 jit_solution(3918131756340966765)
XLA Ops:
  0.6 1.3 %broadcast_in_dim.3.gain_ref = f32[1,768]{1,0:T(1,128)} reshape(f32[768]{0:T(1024)} %param.10) | data formatting | bytes 6144 | tf_op jit(solution)/shard_map/broadcast_in_dim | solution.py:551
  1.9 77.7 %layer.1 = (bf16[1536,768]{1,0:T(8,128)(2,1)}, bf16[1536,768]{1,0:T(8,128)(2,1)}, bf16[1536,768]{1,0:T(8,128)(2,1)}, bf16[1536,768]{1,0:T(8,128)(2,1)}, f32[8,128]{1,0:T(8,128)}) custom-call(bf16[1536,768]{1,0:T(8,128)(2,1)} %q_in.1, bf16[1536,768]{1,0:T(8,128)(2,1)} %k_in.1, bf16[1536,768]{1,0:T(8,128)(2,1)} %v_in.1, bf16[1536,768]{1,0:T(8,128)(2,1)} %do_in.1, ...), custom_call_target="tpu_custom_call" | custom-call | tf_op jit(solution)/shard_map/layer/pallas_call | solution.py:541
  79.6 1.3 %slice_bitcast_fusion = f32[768]{0:T(1024)} fusion(f32[8,128]{1,0:T(8,128)} %get-tuple-element.14), kind=kLoop, calls=%fused_computation | loop fusion | bytes 6144 | tf_op jit(solution)/shard_map/reshape | solution.py:552
  80.8 0.0 copy-start.2
  80.8 3.4 %copy.15 = bf16[1536,768]{1,0:T(8,128)(2,1)} copy(bf16[1536,768]{1,0:T(8,128)(2,1)} %get-tuple-element.20) | data formatting | bytes 4718592
  84.2 0.0 copy-done.2
  84.2 0.0 copy-start.1
  84.2 1.4 %copy.16 = bf16[1536,768]{1,0:T(8,128)(2,1)} copy(bf16[1536,768]{1,0:T(8,128)(2,1)S(1)} %copy-done.2) | data formatting | bytes 4718592
  85.6 1.1 %copy-done.1 = bf16[1536,768]{1,0:T(8,128)(2,1)S(1)} copy-done((bf16[1536,768]{1,0:T(8,128)(2,1)S(1)}, bf16[1536,768]{1,0:T(8,128)(2,1)}, u32[]{:S(2)}) %copy-start.1) | copy-done | bytes 2359320
  86.7 0.0 copy-start
  86.7 1.4 %copy.17 = bf16[1536,768]{1,0:T(8,128)(2,1)} copy(bf16[1536,768]{1,0:T(8,128)(2,1)S(1)} %copy-done.1) | data formatting | bytes 4718592
  88.1 1.1 %copy-done = bf16[1536,768]{1,0:T(8,128)(2,1)S(1)} copy-done((bf16[1536,768]{1,0:T(8,128)(2,1)S(1)}, bf16[1536,768]{1,0:T(8,128)(2,1)}, u32[]{:S(2)}) %copy-start) | copy-done | bytes 2359320
  89.3 1.4 %copy.18 = bf16[1536,768]{1,0:T(8,128)(2,1)} copy(bf16[1536,768]{1,0:T(8,128)(2,1)S(1)} %copy-done) | data formatting | bytes 4718592
Async XLA Ops:
  80.8 3.4 %copy-start.2 = (bf16[1536,768]{1,0:T(8,128)(2,1)S(1)}, bf16[1536,768]{1,0:T(8,128)(2,1)}, u32[]{:S(2)}) copy-start(bf16[1536,768]{1,0:T(8,128)(2,1)} %get-tuple-element.21) | copy-start | bytes 7077892
  84.2 2.5 %copy-start.1 = (bf16[1536,768]{1,0:T(8,128)(2,1)S(1)}, bf16[1536,768]{1,0:T(8,128)(2,1)}, u32[]{:S(2)}) copy-start(bf16[1536,768]{1,0:T(8,128)(2,1)} %get-tuple-element.22) | copy-start | bytes 7077892
  86.7 2.5 %copy-start = (bf16[1536,768]{1,0:T(8,128)(2,1)S(1)}, bf16[1536,768]{1,0:T(8,128)(2,1)}, u32[]{:S(2)}) copy-start(bf16[1536,768]{1,0:T(8,128)(2,1)} %get-tuple-element.23) | copy-start | bytes 7077892
where the time goes:
time: 91 us; the launch traced here: 90.7 us
  Pallas kernels  77.7 us (85%)
  local copies, waits for them, and re-layouts  12.4 us (14%)
    pallas_call x1, Pallas kernels, body(): pl.pallas_call(functools.partial(layer_kernel, shards, head_shards, float...  77.7 us
    unnamed x10, local copies, waits for them, and re-layouts  9.81 us

commit v1 on v0

--- a/solution.py
+++ b/solution.py
@@ -206,11 +206,18 @@
             out_ref[8 * r : 8 * r + 8, GL * half : GL * half + GL] = self.given[o]
 
 
+def rows_of(i):
+    return pl.ds(pl.multiple_of(i * C, C), C)
+
+
+groups = [slice(GL * g, GL * (g + 1)) for g in range(2)]
+
+
 def layer_kernel(
-    shards, head_shards, total_width, chunks, q_in, k_in, v_in, do_in, gain_ref, ld_ref,
-    out_ref, dq_ref, dk_ref, dv_ref, dgain_ref,
-    q_s, k_s, v_s, do_s, in_sems, ct_s, cexp_s, att_s, u_s, shi_s, slo_s, ghi_s, glo_s, ehi_s, elo_s,
-    dv_s, own_s, tot_s, run_s, start_s, dg_s, sums_s, sums_t, sums_sems,
+    shards, head_shards, total_width, chunks, q_in, k_in, v_in, do_in, gain_in, ld_ref,
+    out_ref, dq_ref, k_s, v_s, att_s, dv_s, u_s, cexp_s, run_s, dgain_ref,
+    q_s, do_s, in_sems, ct_s, shi_s, slo_s, ghi_s, glo_s, ehi_s, elo_s,
+    own_s, tot_s, start_s, dg_s, gain_ref, sums_s, sums_t, sums_sems,
     gsend, gtaken, gsems, *scan_refs,
 ):
     remote = shards > 1
@@ -247,11 +254,8 @@
     for a in (2, 3):
         for b in range(PIECES):
             arrival(a, b).start()
-
-    def rows_of(i):
-        return pl.ds(pl.multiple_of(i * C, C), C)
-
-    groups = [slice(GL * g, GL * (g + 1)) for g in range(2)]
+    for j in range(gain_ref.shape[1] // 128):
+        gain_ref[:, 128 * j : 128 * j + 128] = gain_in[128 * j : 128 * j + 128].reshape(1, 128)
 
     row = lax.broadcasted_iota(jnp.int32, (C, C), 0)
     col = lax.broadcasted_iota(jnp.int32, (C, C), 1)
@@ -298,7 +302,9 @@
                 w = window(p)
                 heads = (4 * g + 2 * p, 4 * g + 2 * p + 1)
                 scores = dot_nt(q[:, w], stacked(k[:, w], p)) * pair_decay(ct, cols, heads, bias)
-                outs.append(both(*split(scores), stacked(v[:, w], p)))
+                hi, lo = split(scores)
+                vs = stacked(v[:, w], p)
+                outs.append(dot(hi, vs) + dot(lo, vs))
             att_s[rows, lanes] = merge(*outs)
 
     def whole_rows(i):
@@ -405,25 +411,6 @@
             dk_s[rows, lanes] = merge(*dks)
             dv_s[rows, lanes] = merge(*dvs)
 
-    def last_rows(i):
-        rows = rows_of(i)
-        for g, lanes in enumerate(groups):
-            k, v = k_s[rows, lanes], v_s[rows, lanes]
-            cexp = cexp_s[rows, lanes]
-            end = cexp[C - 1 : C, :]
-            tail = jnp.exp2(end - cexp)
-            s = run_s[:, lanes]
-            s_hi, s_lo = split(s)
-            dks, dvs = [], []
-            for p in range(2):
-                w = window(p)
-                b_hi, b_lo = block_state(s_hi[:, w], p), block_state(s_lo[:, w], p)
-                dks.append(dot_nt(v[:, w], b_hi) + dot_nt(v[:, w], b_lo))
-                dvs.append(dot(k[:, w], b_hi) + dot(k[:, w], b_lo))
-            dk_ref[rows, lanes] = (dk_s[rows, lanes] + tail * merge(*dks)).astype(BF16)
-            dv_ref[rows, lanes] = (dv_s[rows, lanes] + tail * merge(*dvs)).astype(BF16)
-            run_s[:, lanes] = jnp.exp2(end) * s + u_s[i, :, lanes]
-
     def over(lo, hi, f):
         pl.loop(lo, hi)(f)
 
@@ -496,7 +483,55 @@
     else:
         dgain_ref[...] = tile
         run_s[...] = jnp.zeros_like(run_s)
-    over(0, chunks, lambda i: last_rows(chunks - 1 - i))
+
+
+def last_kernel(
+    chunks, out_v, dq_v, k_s, v_s, dk_s, dv_s, u_s, cexp_s, state_ref, dgain_v,
+    out_hbm, dq_hbm, dk_hbm, dv_hbm, dgain_ref, dk_ref, dv_ref, run_s, sems,
+):
+    first = [(out_v, out_hbm), (dq_v, dq_hbm)]
+    for j, (src, dst) in enumerate(first):
+        pltpu.make_async_copy(src, dst, sems.at[j, 0]).start()
+    for j in range(dgain_ref.shape[0] // 128):
+        dgain_ref[128 * j : 128 * j + 128] = dgain_v[j : j + 1, :].reshape(128)
+    run_s[...] = state_ref[...]
+
+    def copies(i):
+        rows = rows_of(i)
+        return [
+            pltpu.make_async_copy(src.at[rows], dst.at[rows], sems.at[2 + j, i])
+            for j, (src, dst) in enumerate([(dk_ref, dk_hbm), (dv_ref, dv_hbm)])
+        ]
+
+    def last_rows(i):
+        rows = rows_of(i)
+        for g, lanes in enumerate(groups):
+            k, v = k_s[rows, lanes], v_s[rows, lanes]
+            cexp = cexp_s[rows, lanes]
+            end = cexp[C - 1 : C, :]
+            tail = jnp.exp2(end - cexp)
+            s = run_s[:, lanes]
+            s_hi, s_lo = split(s)
+            dks, dvs = [], []
+            for p in range(2):
+                w = window(p)
+                b_hi, b_lo = block_state(s_hi[:, w], p), block_state(s_lo[:, w], p)
+                dks.append(dot_nt(v[:, w], b_hi) + dot_nt(v[:, w], b_lo))
+                dvs.append(dot(k[:, w], b_hi) + dot(k[:, w], b_lo))
+            dk_ref[rows, lanes] = (dk_s[rows, lanes] + tail * merge(*dks)).astype(BF16)
+            dv_ref[rows, lanes] = (dv_s[rows, lanes] + tail * merge(*dvs)).astype(BF16)
+            run_s[:, lanes] = jnp.exp2(end) * s + u_s[i, :, lanes]
+        for copy in copies(i):
+            copy.start()
+
+    pl.loop(0, chunks)(lambda i: last_rows(chunks - 1 - i))
+    for j, (src, dst) in enumerate(first):
+        pltpu.make_async_copy(src, dst, sems.at[j, 0]).wait()
+
+    @pl.loop(0, chunks)
+    def _(i):
+        for copy in copies(i):
+            copy.wait()
 
 
 def body(shards, head_shards, queries, keys, values, log_decay, gain, d_out):
@@ -512,21 +547,18 @@
         pltpu.VMEM((OWNERS, 8, GL), F32),
         pltpu.SemaphoreType.DMA((4,)),
     ]
-    scratch = [rows(BF16)] * 4 + [
+    scratch = [
+        rows(BF16), rows(BF16),
         pltpu.SemaphoreType.DMA((4, PIECES)),
         pltpu.VMEM((chunks * 8, C), F32),
-        rows(F32),
-        rows(F32),
-        pltpu.VMEM((chunks, HS, width), F32),
         pltpu.VMEM((chunks, HS, width), BF16),
         pltpu.VMEM((chunks, HS, width), BF16),
         rows(BF16), rows(BF16), rows(BF16), rows(BF16),
-        rows(F32),
         pltpu.VMEM((HS, width), F32),
         pltpu.VMEM((8, 128), F32),
-        pltpu.VMEM((HS, width), F32),
         pltpu.VMEM((8, width), F32),
         pltpu.VMEM((8, width), F32),
+        pltpu.VMEM((1, width), F32),
         pltpu.VMEM((chunks, 8, C), F32),
         pltpu.VMEM((head_shards, chunks, 8, C), F32),
         pltpu.SemaphoreType.DMA((2, PIECES)),
@@ -537,23 +569,37 @@
     params = dict(vmem_limit_bytes=VMEM_LIMIT)
     if shards > 1:
         params.update(collective_id=0, has_side_effects=True)
-    out = OUT((n, width), BF16)
-    outs = pl.pallas_call(
+    held = [rows(BF16)] * 4 + [
+        rows(F32), rows(F32), pltpu.VMEM((chunks, HS, width), F32), rows(F32),
+        pltpu.VMEM((HS, width), F32), pltpu.VMEM((8, 128), F32),
+    ]
+    held = pl.pallas_call(
         functools.partial(
             layer_kernel, shards, head_shards, float(width * head_shards), chunks
         ),
         in_specs=[hbm] * 4 + [vmem, vmem],
-        out_specs=[vmem] * 5,
-        out_shape=[out] * 4 + [jax.ShapeDtypeStruct((8, 128), F32)],
+        out_specs=[vmem] * len(held),
+        out_shape=held,
         scratch_shapes=scratch,
         compiler_params=pltpu.CompilerParams(**params),
         name="layer",
-    )(queries, keys, values, d_out, gain[None], ld_t)
-    return (*outs[:4], outs[4][:6].reshape(width))
-
-
-VMEM_LIMIT = 60 * 1024 * 1024
-OUT = jax.ShapeDtypeStruct
+    )(queries, keys, values, d_out, gain, ld_t)
+    out = jax.ShapeDtypeStruct((n, width), BF16)
+    return pl.pallas_call(
+        functools.partial(last_kernel, chunks),
+        in_specs=[vmem] * len(held),
+        out_specs=[hbm] * 4 + [vmem],
+        out_shape=[out] * 4 + [jax.ShapeDtypeStruct((width,), F32)],
+        scratch_shapes=[
+            rows(BF16), rows(BF16), pltpu.VMEM((HS, width), F32), pltpu.SemaphoreType.DMA((4, chunks))
+        ],
+        compiler_params=pltpu.CompilerParams(vmem_limit_bytes=LAST_LIMIT),
+        name="last",
+    )(*held)
+
+
+VMEM_LIMIT = 30 * 1024 * 1024
+LAST_LIMIT = 12 * 1024 * 1024
 
 
 def solution(mesh):

time: 91 us -> 77.6 us (0.85)
  local copies, waits for them, and re-layouts: 12.4 us -> 0 us
    unnamed x10 -> x0, local copies, waits for them, and re-layouts: 9.81 us -> none
    pallas_call x1, Pallas kernels: 77.7 us -> 68.1 us  [body(): pl.pallas_call(functools.partial(layer_kernel, shards, head_shards, float...]
    pallas_call x0 -> x1, Pallas kernels: none -> 8.64 us  [body(): pl.pallas_call(functools.partial(last_kernel, chunks), in_specs=[vmem] *...]
    reshape x1 -> x0, local copies, waits for them, and re-layouts: 1.28 us -> none  [body(): return (*outs[:4], outs[4][:6].reshape(width))]
    broadcast_in_dim x1 -> x0, local copies, waits for them, and re-layouts: 1.27 us -> none  [body(): gain[None]]
where the time goes in v1:
time: 77.6 us; the launch traced here: 77.4 us
  Pallas kernels  76.8 us (99%)
    pallas_call x1, Pallas kernels, body(): pl.pallas_call(functools.partial(layer_kernel, shards, head_shards, float...  68.1 us
    pallas_call x1, Pallas kernels, body(): pl.pallas_call(functools.partial(last_kernel, chunks), in_specs=[vmem] *...  8.64 us

profile of v1, /device:TPU:1, one launch (start us, length us, event | category | flops | bytes accessed | tf_op | source)
XLA Modules:
  0.0 77.4 jit_solution(12736016106086730276)
XLA Ops:
  0.6 68.1 %layer.1 = (bf16[1536,768]{1,0:T(8,128)(2,1)S(1)}, bf16[1536,768]{1,0:T(8,128)(2,1)S(1)}, bf16[1536,768]{1,0:T(8,128)(2,1)S(1)}, bf16[1536,768]{1,0:T(8,128)(2,1...) custom-call(bf16[1536,768]{1,0:T(8,128)(2,1)} %q_in.1, ...), custom_call_target="tpu_custom_call" | custom-call | tf_op jit(solution)/shard_map/layer/pallas_call | solution.py:576
  68.8 8.6 %last.1 = (bf16[1536,768]{1,0:T(8,128)(2,1)}, bf16[1536,768]{1,0:T(8,128)(2,1)}, bf16[1536,768]{1,0:T(8,128)(2,1)}, bf16[1536,768]{1,0:T(8,128)(2,1)}, f32[768]{0:T(1024)}) custom-call(bf16[1536,768]{1,0:T(8,128)(2,1)S(1)} %get-tuple-element.15.out_v, bf16[1536,768]{1,0:T(8,128)(2,1)S(1)} %get-tuple-element.16.dq_v, ...), custom_call_target="tpu_custom_call" | custom-call | tf_op jit(solution)/shard_map/last/pallas_call | solution.py:588

commit v2 on v1

--- a/solution.py
+++ b/solution.py
@@ -104,11 +104,10 @@
     return slice(128 * parity, 128 * parity + 256)
 
 
-def causal_bias(transposed):
+def causal_bias():
     row = lax.broadcasted_iota(jnp.int32, (C, C), 0)
     col = lax.broadcasted_iota(jnp.int32, (C, C), 1)
-    keep = row <= col if transposed else row >= col
-    return jnp.where(keep, 0.0, NEG)
+    return jnp.where(row >= col, 0.0, NEG)
 
 
 def pair_decay(ct, cols, heads, bias):
@@ -116,9 +115,8 @@
     return jnp.concatenate(parts, axis=1)
 
 
-def pair_decay_t(ct, cols, heads, bias):
-    parts = [jnp.exp2(ct[h : h + 1, :] - cols[h] + bias) for h in heads]
-    return jnp.concatenate(parts, axis=1)
+def turned(x):
+    return jnp.concatenate([x[:, :C].T, x[:, C:].T], axis=1)
 
 
 def token_sums(x):
@@ -216,7 +214,7 @@
 def layer_kernel(
     shards, head_shards, total_width, chunks, q_in, k_in, v_in, do_in, gain_in, ld_ref,
     out_ref, dq_ref, k_s, v_s, att_s, dv_s, u_s, cexp_s, run_s, dgain_ref,
-    q_s, do_s, in_sems, ct_s, shi_s, slo_s, ghi_s, glo_s, ehi_s, elo_s,
+    q_s, do_s, in_sems, ct_s, shi_s, slo_s, ghi_s, glo_s, phi_s, plo_s,
     own_s, tot_s, start_s, dg_s, gain_ref, sums_s, sums_t, sums_sems,
     gsend, gtaken, gsems, *scan_refs,
 ):
@@ -294,7 +292,7 @@
         rows = rows_of(i)
         ct = ct_of(i)
         cols = columns_of(ct)
-        bias = causal_bias(False)
+        bias = causal_bias()
         for g, lanes in enumerate(groups):
             q, k, v = q_s[rows, lanes], k_s[rows, lanes], v_s[rows, lanes]
             outs = []
@@ -305,6 +303,9 @@
                 hi, lo = split(scores)
                 vs = stacked(v[:, w], p)
                 outs.append(dot(hi, vs) + dot(lo, vs))
+                pair = slice(256 * (2 * g + p), 256 * (2 * g + p) + 256)
+                phi_s[rows, pair] = turned(hi)
+                plo_s[rows, pair] = turned(lo)
             att_s[rows, lanes] = merge(*outs)
 
     def whole_rows(i):
@@ -365,8 +366,6 @@
             cexp = cexp_s[rows, lanes]
             end = cexp[C - 1 : C, :]
             e_hi, e_lo = split(grad * jnp.exp2(cexp))
-            ehi_s[rows, lanes] = e_hi
-            elo_s[rows, lanes] = e_lo
             e_both = jnp.concatenate([e_hi, e_lo], axis=0)
             qt = q_s[rows, lanes].T
             parts = []
@@ -382,32 +381,29 @@
         rows = rows_of(i)
         ct = ct_of(i)
         cols = columns_of(ct)
-        bias, bias_t = causal_bias(False), causal_bias(True)
+        bias = causal_bias()
         for g, lanes in enumerate(groups):
             q, k, v = q_s[rows, lanes], k_s[rows, lanes], v_s[rows, lanes]
             g_hi, g_lo = ghi_s[rows, lanes], glo_s[rows, lanes]
-            e_hi, e_lo = ehi_s[rows, lanes], elo_s[rows, lanes]
+            from_start = jnp.exp2(cexp_s[rows, lanes])
             s_hi, s_lo = shi_s[i, :, lanes], slo_s[i, :, lanes]
-            dqs, dks, dvs = [], [], []
+            dqs, olds, dks, dvs = [], [], [], []
             for p in range(2):
                 w = window(p)
                 heads = (4 * g + 2 * p, 4 * g + 2 * p + 1)
-                qw, kw, vw, hw, lw = q[:, w], k[:, w], v[:, w], g_hi[:, w], g_lo[:, w]
-                ks, qs, vs = stacked(kw, p), stacked(qw, p), stacked(vw, p)
+                pair = slice(256 * (2 * g + p), 256 * (2 * g + p) + 256)
+                hw, lw = g_hi[:, w], g_lo[:, w]
                 hs, ls = stacked(hw, p), stacked(lw, p)
                 decay = pair_decay(ct, cols, heads, bias)
-                decay_t = pair_decay_t(ct, cols, heads, bias_t)
                 b_hi, b_lo = block_state(s_hi[:, w], p), block_state(s_lo[:, w], p)
-                d_hi, d_lo = split(both_nt(hw, lw, vs) * decay)
-                dqs.append(
-                    both(d_hi, d_lo, ks)
-                    + (both_nt(e_hi[:, w], e_lo[:, w], b_hi) + dot_nt(e_hi[:, w], b_lo))
-                )
-                t_hi, t_lo = split((dot_nt(vw, hs) + dot_nt(vw, ls)) * decay_t)
-                dks.append(both(t_hi, t_lo, qs))
-                p_hi, p_lo = split(dot_nt(kw, qs) * decay_t)
+                d_hi, d_lo = split(both_nt(hw, lw, stacked(v[:, w], p)) * decay)
+                ks = stacked(k[:, w], p)
+                dqs.append(dot(d_hi, ks) + dot(d_lo, ks))
+                olds.append(both_nt(hw, lw, b_hi) + dot_nt(hw, b_lo))
+                dks.append(both(turned(d_hi), turned(d_lo), stacked(q[:, w], p)))
+                p_hi, p_lo = phi_s[rows, pair], plo_s[rows, pair]
                 dvs.append(both(p_hi, p_lo, hs) + dot(p_hi, ls))
-            dq_ref[rows, lanes] = merge(*dqs).astype(BF16)
+            dq_ref[rows, lanes] = (merge(*dqs) + from_start * merge(*olds)).astype(BF16)
             dk_s[rows, lanes] = merge(*dks)
             dv_s[rows, lanes] = merge(*dvs)
 
@@ -553,7 +549,8 @@
         pltpu.VMEM((chunks * 8, C), F32),
         pltpu.VMEM((chunks, HS, width), BF16),
         pltpu.VMEM((chunks, HS, width), BF16),
-        rows(BF16), rows(BF16), rows(BF16), rows(BF16),
+        rows(BF16), rows(BF16),
+        pltpu.VMEM((n, 1024), BF16), pltpu.VMEM((n, 1024), BF16),
         pltpu.VMEM((HS, width), F32),
         pltpu.VMEM((8, 128), F32),
         pltpu.VMEM((8, width), F32),
@@ -598,7 +595,7 @@
     )(*held)
 
 
-VMEM_LIMIT = 30 * 1024 * 1024
+VMEM_LIMIT = 33 * 1024 * 1024
 LAST_LIMIT = 12 * 1024 * 1024
 
 

time: 77.6 us -> 71.3 us (0.919)
  Pallas kernels: 76.8 us -> 70.5 us
    pallas_call x1, Pallas kernels: 68.1 us -> 61.8 us  [body(): pl.pallas_call(functools.partial(layer_kernel, shards, head_shards, float...]
where the time goes in v2:
time: 71.3 us; the launch traced here: 71.1 us
  Pallas kernels  70.5 us (99%)
    pallas_call x1, Pallas kernels, body(): pl.pallas_call(functools.partial(layer_kernel, shards, head_shards, float...  61.8 us
    pallas_call x1, Pallas kernels, body(): pl.pallas_call(functools.partial(last_kernel, chunks), in_specs=[vmem] *...  8.72 us

profile of v2, /device:TPU:1, one launch (start us, length us, event | category | flops | bytes accessed | tf_op | source)
XLA Modules:
  0.0 71.1 jit_solution(14590467905048408218)
XLA Ops:
  0.6 61.8 %layer.1 = (bf16[1536,768]{1,0:T(8,128)(2,1)S(1)}, bf16[1536,768]{1,0:T(8,128)(2,1)S(1)}, bf16[1536,768]{1,0:T(8,128)(2,1)S(1)}, bf16[1536,768]{1,0:T(8,128)(2,1...) custom-call(bf16[1536,768]{1,0:T(8,128)(2,1)} %q_in.1, ...), custom_call_target="tpu_custom_call" | custom-call | tf_op jit(solution)/shard_map/layer/pallas_call | solution.py:573
  62.4 8.7 %last.1 = (bf16[1536,768]{1,0:T(8,128)(2,1)}, bf16[1536,768]{1,0:T(8,128)(2,1)}, bf16[1536,768]{1,0:T(8,128)(2,1)}, bf16[1536,768]{1,0:T(8,128)(2,1)}, f32[768]{0:T(1024)}) custom-call(bf16[1536,768]{1,0:T(8,128)(2,1)S(1)} %get-tuple-element.15.out_v, bf16[1536,768]{1,0:T(8,128)(2,1)S(1)} %get-tuple-element.16.dq_v, ...), custom_call_target="tpu_custom_call" | custom-call | tf_op jit(solution)/shard_map/last/pallas_call | solution.py:585

commit v3 on v2

--- a/solution.py
+++ b/solution.py
@@ -13,7 +13,7 @@
 HS = 96
 GL = 384
 PIECES = 3
-OWNERS = 24
+OWNERS = HS // 8
 NEG = -1e30
 LOG2E = 1.4426950408889634
 MESH = pl.DeviceIdType.MESH
@@ -130,78 +130,126 @@
     pltpu.make_async_copy(ref, ref, sem).wait()
 
 
-def owner_of(device):
-    return (device // 4) * 3 + jnp.minimum(lax.rem(device, 4), 2)
+def owner_of(chip):
+    y, x = chip // 4, lax.rem(chip, 4)
+    return 3 * y + jnp.minimum(lax.rem(x - y + 3, 4), 2), lax.rem(x - y + 4, 4) != 0
 
 
 class Scan:
-    def __init__(self, count, me, reverse, send, taken, made, given, sems):
-        self.count, self.me, self.reverse = count, me, reverse
-        self.send, self.taken, self.made, self.given, self.sems = send, taken, made, given, sems
-        self.is_owner = lax.rem(me, 4) != 3
-        self.mine = owner_of(me)
-
-    def start(self, state_ref, tot_ref):
-        for o in range(OWNERS):
-            r, half = o // 2, o % 2
-            self.send[o, :, :GL] = state_ref[8 * r : 8 * r + 8, GL * half : GL * half + GL]
-            tot = tot_ref[4 * half : 4 * half + 4, :]
-            self.send[o, :, GL:] = jnp.concatenate([tot, tot], axis=0)
-
-        @pl.loop(1, self.count)
+    def __init__(self, chips, me, reverse, tots, refs):
+        self.chips, self.reverse, self.tots = chips, reverse, tots
+        self.swap, self.swapped, self.send, self.taken, self.made, self.given = refs[:6]
+        self.turn, self.turned, self.sems = refs[6:]
+        self.chip, self.core = me // 2, lax.rem(me, 2)
+        self.mine, self.is_owner = owner_of(self.chip)
+
+    def other_core(self, src, dst, j):
+        return pltpu.make_async_remote_copy(
+            src_ref=src, dst_ref=dst, send_sem=self.sems.at[j], recv_sem=self.sems.at[j + 1],
+            device_id={"ctx": 2 * self.chip + 1 - self.core}, device_id_type=MESH,
+        )
+
+    def other_chip(self, src, dst, j, chip):
+        return pltpu.make_async_remote_copy(
+            src_ref=src, dst_ref=dst, send_sem=self.sems.at[j], recv_sem=self.sems.at[j + 1],
+            device_id={"ctx": 2 * chip + self.core}, device_id_type=MESH,
+        )
+
+    def start(self, state_ref, extra):
+        self.swap[:HS, :] = state_ref[1 - self.core]
+        self.swap[HS:, :] = extra
+        self.other_core(self.swap, self.swapped, 0).start()
+
+    def combine(self, state_ref, extra):
+        self.other_core(self.swap, self.swapped, 0).wait_recv()
+        low = self.core == 0
+        mine, theirs = state_ref[self.core], self.swapped[:HS, :]
+        a, b = jnp.where(low, mine, theirs), jnp.where(low, theirs, mine)
+        ea, eb = jnp.where(low, extra, self.swapped[HS:, :]), jnp.where(low, self.swapped[HS:, :], extra)
+        if self.reverse:
+            both_cores = a + jnp.exp2(self.tots[0, 0:1, :]) * b
+            tile = (ea + eb)[:, :128]
+            self.turn[...] = b
+        else:
+            self.tots[0] = ea
+            self.tots[1] = eb
+            both_cores = jnp.exp2(eb[0:1, :]) * a + b
+            total = ea[0:1, :] + eb[0:1, :]
+            tile = jnp.concatenate(
+                [total[:, 128 * i : 128 * i + 128] for i in range(3)] + [jnp.zeros((5, 128), F32)], axis=0
+            )
+            self.turn[...] = a
+        for r in range(OWNERS):
+            self.send[r, :, :GL] = both_cores[8 * r : 8 * r + 8]
+            self.send[r, :, GL:] = tile
+
+        @pl.loop(1, self.chips)
         def _(i):
-            target = lax.rem(self.me + i, self.count)
-
-            @pl.when(lax.rem(target, 4) != 3)
+            chip = lax.rem(self.chip + i, self.chips)
+            r, owns = owner_of(chip)
+
+            @pl.when(owns)
             def _():
-                pltpu.make_async_remote_copy(
-                    src_ref=self.send.at[owner_of(target)], dst_ref=self.taken.at[self.me],
-                    send_sem=self.sems.at[0], recv_sem=self.sems.at[1],
-                    device_id={"ctx": target}, device_id_type=MESH,
-                ).start()
-
-    def middle(self):
-        count, me, mine = self.count, self.me, self.mine
+                self.other_chip(self.send.at[r], self.taken.at[self.chip], 2, chip).start()
+
+    def middle(self, totals):
+        chips, chip, mine = self.chips, self.chip, self.mine
 
         @pl.when(self.is_owner)
         def _():
-            self.taken[me] = self.send[mine]
-            wait_bytes(self.taken.at[pl.ds(0, count - 1)], self.sems.at[1])
-
-            def step(i, acc):
-                j = count - 1 - i if self.reverse else i
-                self.made[j] = acc
-                rows = [jnp.broadcast_to(self.taken[j, h : h + 1, GL:], (8, 128)) for h in range(4)]
-                return jnp.exp2(group_lanes(rows)) * acc + self.taken[j, :, :GL]
-
-            lax.fori_loop(0, count, step, jnp.zeros((8, GL), F32), unroll=4)
-
-            @pl.loop(1, count)
+            self.taken[chip] = self.send[mine]
+            wait_bytes(self.taken.at[pl.ds(0, chips - 1)], self.sems.at[3])
+
+            def step(i, carry):
+                acc, tile = carry
+                j = chips - 1 - i if self.reverse else i
+                self.made[j, :, :GL] = acc
+                total = jnp.concatenate([totals[j, t : t + 1, GL:] for t in range(3)], axis=1)
+                if self.reverse:
+                    tile = tile + self.taken[j, :, GL:]
+                return jnp.exp2(total) * acc + self.taken[j, :, :GL], tile
+
+            _, tile = lax.fori_loop(
+                0, chips, step, (jnp.zeros((8, GL), F32), jnp.zeros((8, 128), F32)), unroll=4
+            )
+            for j in range(chips):
+                self.made[j, :, GL:] = tile
+
+            @pl.loop(1, chips)
             def _(i):
-                target = lax.rem(me + i, count)
-                pltpu.make_async_remote_copy(
-                    src_ref=self.made.at[target], dst_ref=self.given.at[mine],
-                    send_sem=self.sems.at[2], recv_sem=self.sems.at[3],
-                    device_id={"ctx": target}, device_id_type=MESH,
-                ).start()
-
-            self.given[mine] = self.made[me]
-
-    def finish(self, out_ref):
+                to = lax.rem(chip + i, chips)
+                self.other_chip(self.made.at[to], self.given.at[mine], 4, to).start()
+
+            self.given[mine] = self.made[chip]
+
+    def gather(self, keep):
         @pl.when(self.is_owner)
         def _():
-            wait_bytes(self.given.at[pl.ds(0, OWNERS - 1)], self.sems.at[3])
-            wait_bytes(self.send.at[pl.ds(0, OWNERS - 1)], self.sems.at[0])
-            wait_bytes(self.made.at[pl.ds(0, self.count - 1)], self.sems.at[2])
+            wait_bytes(self.given.at[pl.ds(0, OWNERS - 1)], self.sems.at[5])
+            wait_bytes(self.send.at[pl.ds(0, OWNERS - 1)], self.sems.at[2])
+            wait_bytes(self.made.at[pl.ds(0, self.chips - 1)], self.sems.at[4])
 
         @pl.when(jnp.logical_not(self.is_owner))
         def _():
-            wait_bytes(self.given, self.sems.at[3])
-            wait_bytes(self.send, self.sems.at[0])
-
-        for o in range(OWNERS):
-            r, half = o // 2, o % 2
-            out_ref[8 * r : 8 * r + 8, GL * half : GL * half + GL] = self.given[o]
+            wait_bytes(self.given, self.sems.at[5])
+            wait_bytes(self.send, self.sems.at[2])
+
+        low = self.core == 0
+        outer = jnp.concatenate([self.given[r, :, :GL] for r in range(OWNERS)], axis=0)
+        if self.reverse:
+            inner = self.turn[...] + jnp.exp2(self.tots[1, 0:1, :]) * outer
+            mine, theirs = jnp.where(low, inner, outer), jnp.where(low, outer, inner)
+        else:
+            inner = self.turn[...] + jnp.exp2(self.tots[0, 0:1, :]) * outer
+            mine, theirs = jnp.where(low, outer, inner), jnp.where(low, inner, outer)
+        keep[self.core] = mine
+        self.turn[...] = theirs
+        self.other_core(self.turn, self.turned, 6).start()
+
+    def finish(self, keep):
+        self.other_core(self.turn, self.turned, 6).wait()
+        self.other_core(self.swap, self.swapped, 0).wait_send()
+        keep[1 - self.core] = self.turned[...]
 
 
 def rows_of(i):
@@ -216,20 +264,25 @@
     out_ref, dq_ref, k_s, v_s, att_s, dv_s, u_s, cexp_s, run_s, dgain_ref,
     q_s, do_s, in_sems, ct_s, shi_s, slo_s, ghi_s, glo_s, phi_s, plo_s,
     own_s, tot_s, start_s, dg_s, gain_ref, sums_s, sums_t, sums_sems,
-    gsend, gtaken, gsems, *scan_refs,
+    tots_s, *scan_refs,
 ):
     remote = shards > 1
     dk_s = att_s
     if remote:
         me, my_head = lax.axis_index("ctx"), lax.axis_index("head")
-        on = Scan(shards, me, False, *scan_refs[:5])
-        back = Scan(shards, me, True, *scan_refs[5:])
+        chips = shards // 2
+        core = lax.rem(me, 2)
+        on = Scan(chips, me, False, tots_s, scan_refs[:9])
+        back = Scan(chips, me, True, tots_s, scan_refs[9:])
         barrier = pltpu.get_barrier_semaphore()
-
-        @pl.loop(1, shards)
+        pl.semaphore_signal(
+            barrier, inc=1, device_id={"ctx": me + 1 - 2 * core}, device_id_type=MESH
+        )
+
+        @pl.loop(1, chips)
         def _(i):
             pl.semaphore_signal(
-                barrier, inc=1, device_id={"ctx": lax.rem(me + i, shards)}, device_id_type=MESH
+                barrier, inc=1, device_id={"ctx": lax.rem(me + 2 * i, shards)}, device_id_type=MESH
             )
 
         @pl.loop(1, head_shards)
@@ -286,7 +339,7 @@
                 parts.append(compact(dot(jnp.concatenate([kp, kp], axis=1), v_tail[:, window(p)]), p))
             u = merge(*parts)
             u_s[i, :, lanes] = u
-            own_s[:, lanes] = jnp.exp2(end) * own_s[:, lanes] + u
+            own_s[g] = jnp.exp2(end) * own_s[g] + u
 
     def local_rows(i):
         rows = rows_of(i)
@@ -314,7 +367,7 @@
             q = q_s[rows, lanes]
             cexp = cexp_s[rows, lanes]
             end = cexp[C - 1 : C, :]
-            s = run_s[:, lanes]
+            s = run_s[g]
             s_hi, s_lo = split(s)
             shi_s[i, :, lanes] = s_hi
             slo_s[i, :, lanes] = s_lo
@@ -323,7 +376,7 @@
                 w = window(p)
                 outs.append(dot(q[:, w], block_state(s_hi[:, w], p)) + dot(q[:, w], block_state(s_lo[:, w], p)))
             att_s[rows, lanes] += jnp.exp2(cexp) * merge(*outs)
-            run_s[:, lanes] = jnp.exp2(end) * s + u_s[i, :, lanes]
+            run_s[g] = jnp.exp2(end) * s + u_s[i, :, lanes]
         att = att_s[rows, :]
         grown = do_s[rows, :].astype(F32) * gain_ref[...]
         sums_s[i] = jnp.concatenate(
@@ -374,7 +427,7 @@
                 parts.append(compact(dot(jnp.concatenate([qp, qp], axis=1), e_both[:, window(p)]), p))
             w = merge(*parts)
             u_s[i, :, lanes] = w
-            own_s[:, lanes] += jnp.exp2(start_s[0:1, lanes]) * w
+            own_s[g] += jnp.exp2(start_s[0:1, lanes]) * w
             start_s[0:1, lanes] += end
 
     def grad_rows(i):
@@ -414,17 +467,29 @@
         arrival(0, b).wait()
         arrival(1, b).wait()
         over(b * per, (b + 1) * per, states)
-    if remote:
-        pl.semaphore_wait(barrier, shards + head_shards - 2)
-        on.start(own_s, tot_s)
+    totals = [
+        group_lanes([jnp.broadcast_to(tot_s[h : h + 1, :], (8, 128)) for h in range(4 * g, 4 * g + 4)])
+        for g in range(2)
+    ]
+    if remote:
+        low = core == 0
+        own_total, other_total = jnp.where(low, *totals), jnp.where(low, *totals[::-1])
+        pl.semaphore_wait(barrier, chips + head_shards - 1)
+        on.start(own_s, other_total)
     for b in range(PIECES):
         arrival(2, b).wait()
         arrival(3, b).wait()
-    split_at = chunks // 2
-    over(0, split_at, local_rows)
-    if remote:
-        on.middle()
-    over(split_at, chunks, local_rows)
+    cuts = [chunks * c // 12 for c in LOCAL_CUTS]
+    over(0, cuts[0], local_rows)
+    if remote:
+        on.combine(own_s, own_total)
+    over(cuts[0], cuts[1], local_rows)
+    if remote:
+        on.middle(on.taken)
+    over(cuts[1], cuts[2], local_rows)
+    if remote:
+        on.gather(run_s)
+    over(cuts[2], chunks, local_rows)
     if remote:
         on.finish(run_s)
     else:
@@ -453,28 +518,22 @@
     tile = jnp.concatenate(
         [sums[:, 128 * i : 128 * i + 128] for i in range(6)] + [jnp.zeros((2, 128), F32)], axis=0
     )
-    if remote:
-        back.start(own_s, tot_s)
-        gsend[...] = tile
-        gtaken[me] = tile
-
-        @pl.loop(1, shards)
-        def _(i):
-            pltpu.make_async_remote_copy(
-                src_ref=gsend, dst_ref=gtaken.at[me], send_sem=gsems.at[0], recv_sem=gsems.at[1],
-                device_id={"ctx": lax.rem(me + i, shards)}, device_id_type=MESH,
-            ).start()
-
-    over(0, split_at, grad_rows)
-    if remote:
-        back.middle()
-    over(split_at, chunks, grad_rows)
-    if remote:
-        wait_bytes(gtaken.at[pl.ds(0, shards - 1)], gsems.at[1])
-        wait_bytes(gtaken.at[pl.ds(0, shards - 1)], gsems.at[0])
-        dgain_ref[...] = lax.fori_loop(
-            0, shards, lambda i, acc: acc + gtaken[i], jnp.zeros((8, 128), F32)
-        )
+    cuts = [chunks * c // 12 for c in GRAD_CUTS]
+    if remote:
+        tile = jnp.concatenate([tile, jnp.zeros((8, GL - 128), F32)], axis=1)
+        back.start(own_s, tile)
+    over(0, cuts[0], grad_rows)
+    if remote:
+        back.combine(own_s, tile)
+    over(cuts[0], cuts[1], grad_rows)
+    if remote:
+        back.middle(on.taken)
+    over(cuts[1], cuts[2], grad_rows)
+    if remote:
+        back.gather(run_s)
+        dgain_ref[...] = back.given[0, :, GL:]
+    over(cuts[2], chunks, grad_rows)
+    if remote:
         back.finish(run_s)
     else:
         dgain_ref[...] = tile
@@ -506,7 +565,7 @@
             cexp = cexp_s[rows, lanes]
             end = cexp[C - 1 : C, :]
             tail = jnp.exp2(end - cexp)
-            s = run_s[:, lanes]
+            s = run_s[g]
             s_hi, s_lo = split(s)
             dks, dvs = [], []
             for p in range(2):
@@ -516,7 +575,7 @@
                 dvs.append(dot(k[:, w], b_hi) + dot(k[:, w], b_lo))
             dk_ref[rows, lanes] = (dk_s[rows, lanes] + tail * merge(*dks)).astype(BF16)
             dv_ref[rows, lanes] = (dv_s[rows, lanes] + tail * merge(*dvs)).astype(BF16)
-            run_s[:, lanes] = jnp.exp2(end) * s + u_s[i, :, lanes]
+            run_s[g] = jnp.exp2(end) * s + u_s[i, :, lanes]
         for copy in copies(i):
             copy.start()
 
@@ -536,12 +595,17 @@
     ld_t = log_decay.reshape(chunks, C, 8).transpose(0, 2, 1).reshape(chunks * 8, C)
     hbm, vmem = pl.BlockSpec(memory_space=pl.ANY), pl.BlockSpec(memory_space=pltpu.VMEM)
     rows = lambda dtype: pltpu.VMEM((n, width), dtype)
+    chips = max(shards // 2, 1)
     scan = [
+        pltpu.VMEM((HS + 8, GL), F32),
+        pltpu.VMEM((HS + 8, GL), F32),
         pltpu.VMEM((OWNERS, 8, 512), F32),
-        pltpu.VMEM((shards, 8, 512), F32),
-        pltpu.VMEM((shards, 8, GL), F32),
-        pltpu.VMEM((OWNERS, 8, GL), F32),
-        pltpu.SemaphoreType.DMA((4,)),
+        pltpu.VMEM((chips, 8, 512), F32),
+        pltpu.VMEM((chips, 8, 512), F32),
+        pltpu.VMEM((OWNERS, 8, 512), F32),
+        pltpu.VMEM((HS, GL), F32),
+        pltpu.VMEM((HS, GL), F32),
+        pltpu.SemaphoreType.DMA((8,)),
     ]
     scratch = [
         rows(BF16), rows(BF16),
@@ -551,7 +615,7 @@
         pltpu.VMEM((chunks, HS, width), BF16),
         rows(BF16), rows(BF16),
         pltpu.VMEM((n, 1024), BF16), pltpu.VMEM((n, 1024), BF16),
-        pltpu.VMEM((HS, width), F32),
+        pltpu.VMEM((2, HS, GL), F32),
         pltpu.VMEM((8, 128), F32),
         pltpu.VMEM((8, width), F32),
         pltpu.VMEM((8, width), F32),
@@ -559,16 +623,14 @@
         pltpu.VMEM((chunks, 8, C), F32),
         pltpu.VMEM((head_shards, chunks, 8, C), F32),
         pltpu.SemaphoreType.DMA((2, PIECES)),
-        pltpu.VMEM((8, 128), F32),
-        pltpu.VMEM((shards, 8, 128), F32),
-        pltpu.SemaphoreType.DMA((2,)),
+        pltpu.VMEM((2, 8, GL), F32),
     ] + scan + scan
     params = dict(vmem_limit_bytes=VMEM_LIMIT)
     if shards > 1:
         params.update(collective_id=0, has_side_effects=True)
     held = [rows(BF16)] * 4 + [
         rows(F32), rows(F32), pltpu.VMEM((chunks, HS, width), F32), rows(F32),
-        pltpu.VMEM((HS, width), F32), pltpu.VMEM((8, 128), F32),
+        pltpu.VMEM((2, HS, GL), F32), pltpu.VMEM((8, 128), F32),
     ]
     held = pl.pallas_call(
         functools.partial(
@@ -588,13 +650,15 @@
         out_specs=[hbm] * 4 + [vmem],
         out_shape=[out] * 4 + [jax.ShapeDtypeStruct((width,), F32)],
         scratch_shapes=[
-            rows(BF16), rows(BF16), pltpu.VMEM((HS, width), F32), pltpu.SemaphoreType.DMA((4, chunks))
+            rows(BF16), rows(BF16), pltpu.VMEM((2, HS, GL), F32), pltpu.SemaphoreType.DMA((4, chunks))
         ],
         compiler_params=pltpu.CompilerParams(vmem_limit_bytes=LAST_LIMIT),
         name="last",
     )(*held)
 
 
+LOCAL_CUTS = (2, 6, 10)
+GRAD_CUTS = (1, 5, 9)
 VMEM_LIMIT = 33 * 1024 * 1024
 LAST_LIMIT = 12 * 1024 * 1024
 

time: 71.3 us -> 69.3 us (0.972)
  Pallas kernels: 70.5 us -> 68.3 us
    pallas_call x1, Pallas kernels: 61.8 us -> 59.6 us  [body(): pl.pallas_call(functools.partial(layer_kernel, shards, head_shards, float...]
where the time goes in v3:
time: 69.3 us; the launch traced here: 69.1 us
  Pallas kernels  68.3 us (99%)
  between operations  0.8 us (1%)
    pallas_call x1, Pallas kernels, body(): pl.pallas_call(functools.partial(layer_kernel, shards, head_shards, float...  59.6 us
    pallas_call x1, Pallas kernels, body(): pl.pallas_call(functools.partial(last_kernel, chunks), in_specs=[vmem] *...  8.69 us

profile of v3, /device:TPU:1, one launch (start us, length us, event | category | flops | bytes accessed | tf_op | source)
XLA Modules:
  0.0 69.1 jit_solution(10224675273177033212)
XLA Ops:
  0.6 59.6 %layer.1 = (bf16[1536,768]{1,0:T(8,128)(2,1)S(1)}, bf16[1536,768]{1,0:T(8,128)(2,1)S(1)}, bf16[1536,768]{1,0:T(8,128)(2,1)S(1)}, bf16[1536,768]{1,0:T(8,128)(2,1...) custom-call(bf16[1536,768]{1,0:T(8,128)(2,1)} %q_in.1, ...), custom_call_target="tpu_custom_call" | custom-call | tf_op jit(solution)/shard_map/layer/pallas_call | solution.py:635
  60.3 8.7 %last.1 = (bf16[1536,768]{1,0:T(8,128)(2,1)}, bf16[1536,768]{1,0:T(8,128)(2,1)}, bf16[1536,768]{1,0:T(8,128)(2,1)}, bf16[1536,768]{1,0:T(8,128)(2,1)}, f32[768]{0:T(1024)}) custom-call(bf16[1536,768]{1,0:T(8,128)(2,1)S(1)} %get-tuple-element.15.out_v, bf16[1536,768]{1,0:T(8,128)(2,1)S(1)} %get-tuple-element.16.dq_v, ...), custom_call_target="tpu_custom_call" | custom-call | tf_op jit(solution)/shard_map/last/pallas_call | solution.py:647

commit v4 on v3

--- a/solution.py
+++ b/solution.py
@@ -296,7 +296,7 @@
     inputs = [(k_in, k_s), (v_in, v_s), (q_in, q_s), (do_in, do_s)]
 
     def arrival(a, b):
-        rows = pl.ds(b * per * C, per * C)
+        rows = pl.ds(pl.multiple_of(b * per * C, per * C), per * C)
         return pltpu.make_async_copy(inputs[a][0].at[rows], inputs[a][1].at[rows], in_sems.at[a, b])
 
     for b in range(PIECES):
@@ -461,12 +461,17 @@
             dv_s[rows, lanes] = merge(*dvs)
 
     def over(lo, hi, f):
-        pl.loop(lo, hi)(f)
-
-    for b in range(PIECES):
+        pl.loop(lo, hi, unroll=2 if (hi - lo) % 2 == 0 else 1)(f)
+
+    def piece(b, f):
+        pl.loop(0, per, unroll=per)(lambda j: f(b * per + j))
+
+    @pl.loop(0, PIECES)
+    def _(b):
         arrival(0, b).wait()
         arrival(1, b).wait()
-        over(b * per, (b + 1) * per, states)
+        piece(b, states)
+
     totals = [
         group_lanes([jnp.broadcast_to(tot_s[h : h + 1, :], (8, 128)) for h in range(4 * g, 4 * g + 4)])
         for g in range(2)
@@ -494,8 +499,9 @@
         on.finish(run_s)
     else:
         run_s[...] = jnp.zeros_like(run_s)
-    for b in range(PIECES):
-        over(b * per, (b + 1) * per, whole_rows)
+    @pl.loop(0, PIECES)
+    def _(b):
+        piece(b, whole_rows)
         if remote:
             part = pl.ds(b * per, per)
             sums_t[my_head, part] = sums_s[part]
@@ -507,12 +513,14 @@
     own_s[...] = jnp.zeros_like(own_s)
     start_s[...] = jnp.zeros_like(start_s)
     dg_s[...] = jnp.zeros_like(dg_s)
-    for b in range(PIECES):
+
+    @pl.loop(0, PIECES)
+    def _(b):
         if remote:
             moved = sums_t.at[pl.ds(0, head_shards - 1), pl.ds(b * per, per)]
             wait_bytes(moved, sums_sems.at[1, b])
             wait_bytes(moved, sums_sems.at[0, b])
-        over(b * per, (b + 1) * per, norm_rows)
+        piece(b, norm_rows)
 
     sums = jnp.sum(dg_s[...], axis=0, keepdims=True)
     tile = jnp.concatenate(
@@ -579,7 +587,7 @@
         for copy in copies(i):
             copy.start()
 
-    pl.loop(0, chunks)(lambda i: last_rows(chunks - 1 - i))
+    pl.loop(0, chunks, unroll=3)(lambda i: last_rows(chunks - 1 - i))
     for j, (src, dst) in enumerate(first):
         pltpu.make_async_copy(src, dst, sems.at[j, 0]).wait()
 
@@ -658,7 +666,7 @@
 
 
 LOCAL_CUTS = (2, 6, 10)
-GRAD_CUTS = (1, 5, 9)
+GRAD_CUTS = (2, 6, 10)
 VMEM_LIMIT = 33 * 1024 * 1024
 LAST_LIMIT = 12 * 1024 * 1024
 

time: 69.3 us -> 61.4 us (0.89)
  Pallas kernels: 68.3 us -> 60.5 us
    pallas_call x1, Pallas kernels: 59.6 us -> 52.8 us  [body(): pl.pallas_call(functools.partial(layer_kernel, shards, head_shards, float...]
    pallas_call x1, Pallas kernels: 8.69 us -> 7.69 us  [body(): pl.pallas_call(functools.partial(last_kernel, chunks), in_specs=[vmem] *...]
where the time goes in v4:
time: 61.4 us; the launch traced here: 61.3 us
  Pallas kernels  60.5 us (99%)
  between operations  0.82 us (1%)
    pallas_call x1, Pallas kernels, body(): pl.pallas_call(functools.partial(layer_kernel, shards, head_shards, float...  52.8 us
    pallas_call x1, Pallas kernels, body(): pl.pallas_call(functools.partial(last_kernel, chunks), in_specs=[vmem] *...  7.69 us

profile of v4, /device:TPU:1, one launch (start us, length us, event | category | flops | bytes accessed | tf_op | source)
XLA Modules:
  0.0 61.3 jit_solution(768253695515078638)
XLA Ops:
  0.6 52.8 %layer.1 = (bf16[1536,768]{1,0:T(8,128)(2,1)S(1)}, bf16[1536,768]{1,0:T(8,128)(2,1)S(1)}, bf16[1536,768]{1,0:T(8,128)(2,1)S(1)}, bf16[1536,768]{1,0:T(8,128)(2,1...) custom-call(bf16[1536,768]{1,0:T(8,128)(2,1)} %q_in.1, ...), custom_call_target="tpu_custom_call" | custom-call | tf_op jit(solution)/shard_map/layer/pallas_call | solution.py:643
  53.4 7.7 %last.1 = (bf16[1536,768]{1,0:T(8,128)(2,1)}, bf16[1536,768]{1,0:T(8,128)(2,1)}, bf16[1536,768]{1,0:T(8,128)(2,1)}, bf16[1536,768]{1,0:T(8,128)(2,1)}, f32[768]{0:T(1024)}) custom-call(bf16[1536,768]{1,0:T(8,128)(2,1)S(1)} %get-tuple-element.15.out_v, bf16[1536,768]{1,0:T(8,128)(2,1)S(1)} %get-tuple-element.16.dq_v, ...), custom_call_target="tpu_custom_call" | custom-call | tf_op jit(solution)/shard_map/last/pallas_call | solution.py:655

commit v5 on v4

--- a/solution.py
+++ b/solution.py
@@ -210,10 +210,11 @@
                 return jnp.exp2(total) * acc + self.taken[j, :, :GL], tile
 
             _, tile = lax.fori_loop(
-                0, chips, step, (jnp.zeros((8, GL), F32), jnp.zeros((8, 128), F32)), unroll=4
+                0, chips, step, (jnp.zeros((8, GL), F32), jnp.zeros((8, 128), F32)), unroll=16
             )
-            for j in range(chips):
-                self.made[j, :, GL:] = tile
+            if self.reverse:
+                for j in range(chips):
+                    self.made[j, :, GL:] = tile
 
             @pl.loop(1, chips)
             def _(i):
@@ -264,7 +265,7 @@
     out_ref, dq_ref, k_s, v_s, att_s, dv_s, u_s, cexp_s, run_s, dgain_ref,
     q_s, do_s, in_sems, ct_s, shi_s, slo_s, ghi_s, glo_s, phi_s, plo_s,
     own_s, tot_s, start_s, dg_s, gain_ref, sums_s, sums_t, sums_sems,
-    tots_s, *scan_refs,
+    qt_s, tots_s, *scan_refs,
 ):
     remote = shards > 1
     dk_s = att_s
@@ -321,14 +322,18 @@
     def ct_of(i):
         return ct_s[pl.ds(pl.multiple_of(i * 8, 8), 8), :]
 
-    def states(i):
+    def exponents(i):
         rows = rows_of(i)
         ct = ct_of(i)
         tot_s[...] += jnp.broadcast_to(ct[:, C - 1 : C], (8, 128))
         cols = columns_of(ct)
         for g, lanes in enumerate(groups):
-            cexp = group_lanes(cols[4 * g : 4 * g + 4])
-            cexp_s[rows, lanes] = cexp
+            cexp_s[rows, lanes] = group_lanes(cols[4 * g : 4 * g + 4])
+
+    def states(i):
+        rows = rows_of(i)
+        for g, lanes in enumerate(groups):
+            cexp = cexp_s[rows, lanes]
             end = cexp[C - 1 : C, :]
             v_hi, v_lo = split(v_s[rows, lanes].astype(F32) * jnp.exp2(end - cexp))
             v_tail = jnp.concatenate([v_hi, v_lo], axis=0)
@@ -348,6 +353,7 @@
         bias = causal_bias()
         for g, lanes in enumerate(groups):
             q, k, v = q_s[rows, lanes], k_s[rows, lanes], v_s[rows, lanes]
+            qt_s[i, lanes, :] = q.T
             outs = []
             for p in range(2):
                 w = window(p)
@@ -420,7 +426,7 @@
             end = cexp[C - 1 : C, :]
             e_hi, e_lo = split(grad * jnp.exp2(cexp))
             e_both = jnp.concatenate([e_hi, e_lo], axis=0)
-            qt = q_s[rows, lanes].T
+            qt = qt_s[i, lanes, :]
             parts = []
             for p in range(2):
                 qp = qt[192 * p : 192 * p + 192]
@@ -466,6 +472,8 @@
     def piece(b, f):
         pl.loop(0, per, unroll=per)(lambda j: f(b * per + j))
 
+    pl.loop(0, PIECES)(lambda b: piece(b, exponents))
+
     @pl.loop(0, PIECES)
     def _(b):
         arrival(0, b).wait()
@@ -604,13 +612,13 @@
     hbm, vmem = pl.BlockSpec(memory_space=pl.ANY), pl.BlockSpec(memory_space=pltpu.VMEM)
     rows = lambda dtype: pltpu.VMEM((n, width), dtype)
     chips = max(shards // 2, 1)
-    scan = [
+    scan = lambda sent: [
         pltpu.VMEM((HS + 8, GL), F32),
         pltpu.VMEM((HS + 8, GL), F32),
         pltpu.VMEM((OWNERS, 8, 512), F32),
         pltpu.VMEM((chips, 8, 512), F32),
-        pltpu.VMEM((chips, 8, 512), F32),
-        pltpu.VMEM((OWNERS, 8, 512), F32),
+        pltpu.VMEM((chips, 8, sent), F32),
+        pltpu.VMEM((OWNERS, 8, sent), F32),
         pltpu.VMEM((HS, GL), F32),
         pltpu.VMEM((HS, GL), F32),
         pltpu.SemaphoreType.DMA((8,)),
@@ -631,8 +639,9 @@
         pltpu.VMEM((chunks, 8, C), F32),
         pltpu.VMEM((head_shards, chunks, 8, C), F32),
         pltpu.SemaphoreType.DMA((2, PIECES)),
+        pltpu.VMEM((chunks, width, C), BF16),
         pltpu.VMEM((2, 8, GL), F32),
-    ] + scan + scan
+    ] + scan(GL) + scan(512)
     params = dict(vmem_limit_bytes=VMEM_LIMIT)
     if shards > 1:
         params.update(collective_id=0, has_side_effects=True)
@@ -667,7 +676,7 @@
 
 LOCAL_CUTS = (2, 6, 10)
 GRAD_CUTS = (2, 6, 10)
-VMEM_LIMIT = 33 * 1024 * 1024
+VMEM_LIMIT = 35 * 1024 * 1024
 LAST_LIMIT = 12 * 1024 * 1024
 
 

time: 61.4 us -> 60.7 us (0.989)
  Pallas kernels: 60.5 us -> 59.7 us
    pallas_call x1, Pallas kernels: 52.8 us -> 52 us  [body(): pl.pallas_call(functools.partial(layer_kernel, shards, head_shards, float...]
where the time goes in v5:
time: 60.7 us; the launch traced here: 60.5 us
  Pallas kernels  59.7 us (98%)
  between operations  0.82 us (1%)
    pallas_call x1, Pallas kernels, body(): pl.pallas_call(functools.partial(layer_kernel, shards, head_shards, float...  52 us
    pallas_call x1, Pallas kernels, body(): pl.pallas_call(functools.partial(last_kernel, chunks), in_specs=[vmem] *...  7.68 us

profile of v5, /device:TPU:1, one launch (start us, length us, event | category | flops | bytes accessed | tf_op | source)
XLA Modules:
  0.0 60.5 jit_solution(13247155243882726859)
XLA Ops:
  0.6 52.0 %layer.1 = (bf16[1536,768]{1,0:T(8,128)(2,1)S(1)}, bf16[1536,768]{1,0:T(8,128)(2,1)S(1)}, bf16[1536,768]{1,0:T(8,128)(2,1)S(1)}, bf16[1536,768]{1,0:T(8,128)(2,1...) custom-call(bf16[1536,768]{1,0:T(8,128)(2,1)} %q_in.1, ...), custom_call_target="tpu_custom_call" | custom-call | tf_op jit(solution)/shard_map/layer/pallas_call | solution.py:652
  52.6 7.7 %last.1 = (bf16[1536,768]{1,0:T(8,128)(2,1)}, bf16[1536,768]{1,0:T(8,128)(2,1)}, bf16[1536,768]{1,0:T(8,128)(2,1)}, bf16[1536,768]{1,0:T(8,128)(2,1)}, f32[768]{0:T(1024)}) custom-call(bf16[1536,768]{1,0:T(8,128)(2,1)S(1)} %get-tuple-element.15.out_v, bf16[1536,768]{1,0:T(8,128)(2,1)S(1)} %get-tuple-element.16.dq_v, ...), custom_call_target="tpu_custom_call" | custom-call | tf_op jit(solution)/shard_map/last/pallas_call | solution.py:664

commit v6 on v5

--- a/solution.py
+++ b/solution.py
@@ -674,7 +674,7 @@
     )(*held)
 
 
-LOCAL_CUTS = (2, 6, 10)
+LOCAL_CUTS = (2, 6, 12)
 GRAD_CUTS = (2, 6, 10)
 VMEM_LIMIT = 35 * 1024 * 1024
 LAST_LIMIT = 12 * 1024 * 1024

time: 60.7 us -> 60.7 us (level)
  no operation moved by 1% of the time
where the time goes in v6:
time: 60.7 us; the launch traced here: 60.5 us
  Pallas kernels  59.7 us (98%)
  between operations  0.82 us (1%)
    pallas_call x1, Pallas kernels, body(): pl.pallas_call(functools.partial(layer_kernel, shards, head_shards, float...  52 us
    pallas_call x1, Pallas kernels, body(): pl.pallas_call(functools.partial(last_kernel, chunks), in_specs=[vmem] *...  7.69 us

profile of v6, /device:TPU:1, one launch (start us, length us, event | category | flops | bytes accessed | tf_op | source)
XLA Modules:
  0.0 60.5 jit_solution(8163535675980991579)
XLA Ops:
  0.6 52.0 %layer.1 = (bf16[1536,768]{1,0:T(8,128)(2,1)S(1)}, bf16[1536,768]{1,0:T(8,128)(2,1)S(1)}, bf16[1536,768]{1,0:T(8,128)(2,1)S(1)}, bf16[1536,768]{1,0:T(8,128)(2,1...) custom-call(bf16[1536,768]{1,0:T(8,128)(2,1)} %q_in.1, ...), custom_call_target="tpu_custom_call" | custom-call | tf_op jit(solution)/shard_map/layer/pallas_call | solution.py:652
  52.6 7.7 %last.1 = (bf16[1536,768]{1,0:T(8,128)(2,1)}, bf16[1536,768]{1,0:T(8,128)(2,1)}, bf16[1536,768]{1,0:T(8,128)(2,1)}, bf16[1536,768]{1,0:T(8,128)(2,1)}, f32[768]{0:T(1024)}) custom-call(bf16[1536,768]{1,0:T(8,128)(2,1)S(1)} %get-tuple-element.15.out_v, bf16[1536,768]{1,0:T(8,128)(2,1)S(1)} %get-tuple-element.16.dq_v, ...), custom_call_target="tpu_custom_call" | custom-call | tf_op jit(solution)/shard_map/last/pallas_call | solution.py:664
